TPU v7x, 512 devices: a whole 4x4x16 slice. The times are simulated.
512 devices in a mesh: dp: 128 (over x, y, z_lo), grad: 4 (over z_hi, core).
Axes of the slice: x: 4, y: 4, z: 16 (z_hi: 2, z_lo: 8; z = z_hi * 8 + z_lo), core: 2. Of those that a mesh axis runs over, the one named last changes fastest.
Arguments:
- activations: bfloat16 [1024, 6144], P('grad', 'dp'), may hold values from -6 to 6
- output_grads: bfloat16 [1024, 6144], P('grad', 'dp'), may hold values from -0.1875 to 0.1875
- output_inverse: bfloat16 [6144, 3072], P('dp'), may hold values from -0.078125 to 0.078125
- input_inverse: bfloat16 [6144, 6144], P('dp'), may hold values from -0.078125 to 0.078125
- owner_table: int32 [128], replicated, may hold values from 0 to 127, each once
- factor_slab: float32 [6144, 6144], P('grad', 'dp'), may hold values from -6 to 6
- momentum: float32 [6144, 3072], P('dp', 'grad'), may hold values from -6 to 6
Outputs:
- new_momentum: float32 [6144, 3072], P('dp', 'grad')
- new_factor: float32 [6144, 6144], P('grad', 'dp')
Inputs may be any that keep to these rules, and one draw needn't show every extreme that they name: owner_table is a permutation: every natural feature block is stored exactly once.
All inputs are finite; a program needn't handle non-finite values.
Results may differ from a plain program's by a relative error of at most 0.007.
Values may be sent and summed in bfloat16 or wider, within the bound.
A program may use at most 64 MiB of HBM per device.

v0:
```python
import jax
import jax.numpy as jnp
from jax import lax
from jax.sharding import PartitionSpec as P


def shards(
    activations, output_grads, output_inverse, input_inverse, owner_table, factor_slab, momentum
):
    block_rows = activations.shape[1]
    count_dp = owner_table.shape[0]
    full_width = input_inverse.shape[1]
    total_tokens = activations.shape[0] * lax.axis_size("grad")
    partial_proj = jnp.dot(output_grads, output_inverse, preferred_element_type=jnp.float32)
    projected = lax.psum(partial_proj, "dp").astype(jnp.bfloat16)
    gathered = lax.all_gather(activations, "dp", axis=1, tiled=True)
    columns = gathered
    own_cov = lax.psum_scatter(
        lax.dot_general(
            columns, activations, (((0,), (0,)), ((), ())), preferred_element_type=jnp.float32
        ),
        "grad",
        scatter_dimension=0,
        tiled=True,
    )
    new_factor = 0.2 * factor_slab + 0.8 * (own_cov / total_tokens)
    inverse_stored = input_inverse.reshape(block_rows, count_dp, full_width // count_dp)[
        :, owner_table, :
    ].reshape(block_rows, full_width)
    partial_grad = lax.dot_general(
        activations, projected, (((0,), (0,)), ((), ())), preferred_element_type=jnp.float32
    )
    grad_tile = lax.psum_scatter(partial_grad, "grad", scatter_dimension=1, tiled=True).astype(
        jnp.bfloat16
    )
    columns = inverse_stored
    preconditioned = jnp.dot(
        columns,
        lax.all_gather(grad_tile, "dp", axis=0, tiled=True),
        preferred_element_type=jnp.float32,
    )
    new_momentum = 0.9 * momentum + preconditioned
    return (new_momentum, new_factor)


def solution(mesh):
    return jax.shard_map(
        shards,
        mesh=mesh,
        in_specs=(
            P("grad", "dp"),
            P("grad", "dp"),
            P("dp", None),
            P("dp", None),
            P(),
            P("grad", "dp"),
            P("dp", "grad"),
        ),
        out_specs=(P("dp", "grad"), P("grad", "dp")),
        check_vma=False,
    )
```

profile of v0, /device:TPU:256, one launch (start us, length us, event | category | flops | bytes accessed | tf_op | source)
XLA Modules:
  0.0 2183.6 jit_solution(5282985210781487805)
XLA Ops:
  8.0 0.0 copy-start
  8.0 0.0 all-gather.5.cloned.1.call-start
  8.1 0.7 all-gather.5.cloned.1.call-update
  8.7 0.0 reduce-scatter.3.cloned.1.call-start
  8.8 0.2 copy-done
  9.0 1.3 fusion.1
  10.3 0.0 copy-start.3
  10.3 1093.7 %all-reduce.1 = bf16[256,3072]{1,0:T(8,128)(2,1)} all-reduce(f32[256,3072]{1,0:T(8,128)S(1)} %fusion.1), channel_id=1, replica_groups=mesh['dp'=128,'grad'=4] {'dp'}, use_global_device_ids=true, to_apply=%region_0.0 | all-reduce | flops 786432 | bytes 4718592 | tf_op jit(solution)/shard_map/psum | solution.py:15
  1104.0 2.6 convolution_bitcast_fusion
  1106.6 0.0 reduce-scatter.3.cloned.1.call-update
  1106.7 0.0 reduce-scatter.5.cloned.1.call-start
  1106.7 0.0 all-gather.5.cloned.1.call-done
  1106.7 3.9 fusion.2
  1110.7 0.0 reduce-scatter.5.cloned.1.call-update
  1110.7 0.0 all-gather.3.cloned.1.call-start
  1110.8 42.0 %reduce-scatter.3.cloned.1.call-done = f32[48,768]{1,0:T(8,128)} async-done(((f32[48,3072]{1,0:T(8,128)}), f32[48,768]{1,0:T(8,128)}) %reduce-scatter.3.cloned.1.call-update) | async-done | bytes 147472 | tf_op jit(solution)/shard_map/reduce_scatter | solution.py:33
  1152.8 1.6 convert_element_type.7
  1154.3 0.0 all-gather.3.cloned.1.call-update
  1154.4 1.6 reshape.10
  1156.0 0.0 copy-start.5
  1156.0 1.0 copy.11
  1157.0 0.0 copy-done.5
  1157.1 0.9 gather_fusion
  1157.9 0.4 copy.12
  1158.4 0.0 copy-start.2
  1158.4 0.0 copy-start.4
  1158.4 2.9 reshape.11
  1161.2 50.0 %reduce-scatter.5.cloned.1.call-done = f32[1536,48]{0,1:T(8,128)} async-done(((f32[6144,48]{0,1:T(8,128)}), f32[1536,48]{0,1:T(8,128)}) %reduce-scatter.5.cloned.1.call-update) | async-done | bytes 294928 | tf_op jit(solution)/shard_map/reduce_scatter | solution.py:18
  1211.3 0.0 copy-done.2
  1211.3 1.7 multiply_add_fusion
  1213.0 957.1 %all-gather.3.cloned.1.call-done = bf16[6144,768]{1,0:T(8,128)(2,1)} async-done(((bf16[48,768]{1,0:T(8,128)(2,1)}), bf16[6144,768]{1,0:T(8,128)(2,1)}) %all-gather.3.cloned.1.call-update) | async-done | bytes 9437200 | tf_op jit(solution)/shard_map/all_gather | solution.py:39
  2170.1 6.0 convolution_add_fusion
  (6 shorter events, 0.0 us)
Async XLA Ops:
  8.0 1.0 copy-start
  8.0 1098.7 %all-gather.5.cloned.1.call-start = ((), (), s32[]{:S(2)}) async-start(), calls=%async_computation.4 | async-start | bytes 3170304 | tf_op jit(solution)/shard_map/all_gather | solution.py:16
  8.7 1144.0 %reduce-scatter.3.cloned.1.call-start = ((), (), s32[]{:S(2)}) async-start(), calls=%async_computation.2 | async-start | bytes 737280 | tf_op jit(solution)/shard_map/reduce_scatter | solution.py:33
  10.3 1093.7 %copy-start.3 = (bf16[256,48]{0,1:T(8,128)(2,1)S(1)}, bf16[256,48]{0,1:T(8,128)(2,1)}, u32[]{:S(2)}) copy-start(bf16[256,48]{0,1:T(8,128)(2,1)} %param.7) | copy-start | bytes 73732
  1106.7 104.6 %reduce-scatter.5.cloned.1.call-start = ((), (), s32[]{:S(2)}) async-start(), calls=%async_computation.5 | async-start | bytes 1474560 | tf_op jit(solution)/shard_map/reduce_scatter | solution.py:18
  1110.7 43.7 %copy-start.1 = (bf16[48,6144]{1,0:T(8,128)(2,1)S(1)}, bf16[48,6144]{1,0:T(8,128)(2,1)}, u32[]{:S(2)}) copy-start(bf16[48,6144]{1,0:T(8,128)(2,1)} %param.10) | copy-start | bytes 1769476
  1110.7 1059.4 %all-gather.3.cloned.1.call-start = ((), (), s32[]{:S(2)}) async-start(), calls=%async_computation.3 | async-start | bytes 9510912 | tf_op jit(solution)/shard_map/all_gather | solution.py:39
  1156.0 1.0 copy-start.5
  1158.4 52.9 %copy-start.2 = (f32[1536,48]{0,1:T(8,128)S(1)}, f32[1536,48]{0,1:T(8,128)}, u32[]{:S(2)}) copy-start(f32[1536,48]{0,1:T(8,128)} %param.12) | copy-start | bytes 884740
  1158.4 1011.8 %copy-start.4 = (f32[48,768]{1,0:T(8,128)S(1)}, f32[48,768]{1,0:T(8,128)}, u32[]{:S(2)}) copy-start(f32[48,768]{1,0:T(8,128)} %param.13) | copy-start | bytes 442372
Sparse Core Ops, SparseCore 0:
  10.9 967.4 all-gather.4
  1154.5 1015.6 all-gather.2
Sparse Core Ops, SparseCore 1:
  1106.8 46.0 reduce-scatter.2
  1155.8 55.5 reduce-scatter.4
where the time goes:
time: 2180 us
  blocking collectives  1090 us (50%)
  waiting for transfers between devices  1050 us (48%)
    psum x1, blocking collectives, shards(): projected = lax.psum(partial_proj, 'dp').astype(jnp.bfloat16)  1090 us
    all_gather x1, waiting for transfers between devices, shards(): lax.all_gather(grad_tile, 'dp', axis=0, tiled=True)  957 us
    reduce_scatter x1, waiting for transfers between devices, shards(): lax.psum_scatter(lax.dot_general(columns, activations, (((0,), (0,)), (()...  50 us
  transfers between devices with their start and end apart: 4, of which 3 were waited for; matrix products, arithmetic and copies ran while one was open for 1% of the time, Pallas kernels for 0%

commit v1 on v0

v1 whole, which is shorter than its diff:
```python
import functools

import jax
import jax.numpy as jnp
from jax import lax
from jax.experimental import pallas as pl
from jax.experimental.pallas import tpu as pltpu
from jax.sharding import PartitionSpec as P

MESH = pl.DeviceIdType.MESH
BF = jnp.bfloat16
F32 = jnp.float32
NX, NY, NL = 4, 4, 8
BR = 48
TK = 256
SLAB = 1536
CH = NL * BR
CG = 768
Z_ORDER = (1, 7, 2, 6, 3, 5, 4)


def kernel(
    at, gt, ainv, oinv, fac, mom, out_m, out_f,
    ra, rg, lhs, ai, oi, cvf, cs, cr, yp, yc, yhs, yhr, yb,
    pp, pys, pyr, pa, pls, plr, pq, pf, mf, ms, mr,
    loc, t0s, t0r, fws, fwr, zs, ys, lr, ais, air, ois, oir, cvs, cvr, yss, ysr,
    pyss, pysr, plss, plsr, pfzs, pfys, pfr, mss, msr,
):
    dp = lax.axis_index("dp")
    g = lax.axis_index("grad")
    x = lax.div(dp, 32)
    y = lax.rem(lax.div(dp, 8), 4)
    l = lax.rem(dp, 8)
    h = lax.div(g, 2)
    c = lax.rem(g, 2)

    def dev(x_=None, y_=None, l_=None, h_=None, c_=None):
        x_ = x if x_ is None else x_
        y_ = y if y_ is None else y_
        l_ = l if l_ is None else l_
        h_ = h if h_ is None else h_
        c_ = c if c_ is None else c_
        return ((x_ * NY + y_) * NL + l_, h_ * 2 + c_)

    def rows(i, n):
        return pl.ds(pl.multiple_of(i * n, 16), n)

    def lanes(i, n):
        return pl.ds(pl.multiple_of(i * n, 128), n)

    pending = []

    def send(src, dst, ss, rs, to):
        cp = pltpu.make_async_remote_copy(
            src_ref=src, dst_ref=dst, send_sem=ss, recv_sem=rs, device_id=to, device_id_type=MESH
        )
        cp.start()
        pending.append(cp)

    def arrived(dst, sem):
        pltpu.make_async_copy(dst, dst, sem).wait()

    xk = [lax.rem(x + k, NX) for k in range(NX)]
    yk = [lax.rem(y + k, NY) for k in range(NY)]
    lk = [lax.rem(l + k, NL) for k in range(NL)]

    own_o = pltpu.make_async_copy(oinv.at[:, lanes(g, CG)], oi.at[rows(x, BR)], loc.at[0])
    own_o.start()
    own_a = pltpu.make_async_copy(ainv, ai.at[rows(x, BR)], loc.at[1])
    own_a.start()

    bar = pltpu.get_barrier_semaphore()

    def greet(to):
        pl.semaphore_signal(bar, inc=1, device_id=to, device_id_type=MESH)

    greet(dev(c_=1 - c))
    greet(dev(h_=1 - h))
    for k in range(1, NL):
        greet(dev(l_=lk[k]))
    for k in range(1, NX):
        greet(dev(x_=xk[k]))
        greet(dev(y_=yk[k]))
    for j in range(2):
        x0 = c + 2 * j

        @pl.when(jnp.logical_or(x0 != x, x != g))
        def _():
            greet(dev(x_=x0, h_=lax.div(x, 2), c_=lax.rem(x, 2)))

    pl.semaphore_wait(bar, 17 - jnp.where(x == g, 1, 0))

    cc = lax.rem(x, 2)
    xj = lax.div(x, 2)
    t0 = []
    for a, (src, dst) in enumerate(((at, ra), (gt, rg))):
        near = pltpu.make_async_remote_copy(
            src_ref=src, dst_ref=dst.at[rows(x, BR)], send_sem=t0s.at[a, 0], recv_sem=t0r.at[a, xj],
            device_id=dev(x_=g, c_=cc), device_id_type=MESH,
        )
        far = pltpu.make_async_remote_copy(
            src_ref=src, dst_ref=dst.at[rows(x, BR)], send_sem=t0s.at[a, 1], recv_sem=t0r.at[a, xj],
            device_id=dev(x_=g, h_=1 - h, c_=cc), device_id_type=MESH,
        )
        here = pltpu.make_async_copy(src, dst.at[rows(x, BR)], t0r.at[a, xj])
        far.start()

        @pl.when(x != g)
        def _(near=near):
            near.start()

        @pl.when(x == g)
        def _(here=here):
            here.start()

        t0.append(near)
        pending.append(far)

    own_o.wait()
    for k in range(1, NX):
        r = rows(x, BR)
        send(oi.at[r], oi.at[r], ois.at[k - 1], oir.at[k - 1], dev(x_=xk[k]))
    own_a.wait()
    for k in range(1, NX):
        r = rows(x, BR)
        send(ai.at[r], ai.at[r], ais.at[k - 1], air.at[k - 1], dev(x_=xk[k]))

    def x_from(k):
        return lax.rem(x + (NX - k), NX)

    def y_from(k):
        return lax.rem(y + (NY - k), NY)

    def l_from(k):
        return lax.rem(l + (NL - k), NL)

    blk = ra.at[rows(g, BR)]
    mine = rows(y * NL + l, BR)
    arrived(blk, t0r.at[0, h])
    for k in Z_ORDER:
        send(blk, lhs.at[mine], zs.at[k - 1], lr.at[y * NL + l], dev(l_=lk[k]))
    for k in range(1, NY):
        send(blk, lhs.at[mine], ys.at[0, k - 1], lr.at[y * NL + l], dev(y_=yk[k]))
    lhs[mine, :] = ra[rows(g, BR), :]
    send(blk, blk, fws.at[0, 0], fwr.at[0, h], dev(c_=1 - c))
    other = ra.at[rows(c + 2 * (1 - h), BR)]
    arrived(other, t0r.at[0, 1 - h])
    send(other, other, fws.at[0, 1], fwr.at[0, 1 - h], dev(c_=1 - c))

    for j in range(2):
        b = rg.at[rows(c + 2 * j, BR)]
        arrived(b, t0r.at[1, j])
        send(b, b, fws.at[1, j], fwr.at[1, j], dev(c_=1 - c))
    for j in range(2):
        arrived(rg.at[rows(1 - c + 2 * j, BR)], fwr.at[1, j])
    for k in range(1, NX):
        arrived(oi.at[rows(x_from(k), BR)], oir.at[k - 1])
    gm = rg[...].astype(F32).T.astype(BF)
    part = jnp.dot(gm, oi[...], preferred_element_type=F32)
    pp[...] = part
    pys[...] = part.astype(BF)
    for k in range(1, NY):
        send(pys.at[rows(yk[k], 64)], pyr.at[k - 1], pyss.at[k - 1], pysr.at[k - 1], dev(y_=yk[k]))

    for k in Z_ORDER:
        i = y * NL + l_from(k)
        arrived(lhs.at[rows(i, BR)], lr.at[i])
        for q in range(1, NY):
            send(lhs.at[rows(i, BR)], lhs.at[rows(i, BR)], ys.at[k, q - 1], lr.at[i], dev(y_=yk[q]))

    for k in range(1, NY):
        arrived(pyr.at[k - 1], pysr.at[k - 1])
    acc = pp[rows(y, 64), :]
    for k in range(1, NY):
        acc = acc + pyr[k - 1].astype(F32)
    pa[...] = acc
    pls[...] = acc.astype(BF)

    def piece(l_):
        return rows(lax.div(l_, 2), 16), lanes(lax.rem(l_, 2), 384)

    for k in Z_ORDER:
        r, q = piece(lk[k])
        send(pls.at[r, q], plr.at[k - 1], plss.at[k - 1], plsr.at[k - 1], dev(l_=lk[k]))

    for j in range(2):
        arrived(ra.at[rows(1 - c + 2 * j, BR)], fwr.at[0, j])
    for k in range(1, NX):
        arrived(ai.at[rows(x_from(k), BR)], air.at[k - 1])

    def chunk(j, first):
        yy = y_from(j)
        f = lhs[rows(yy, CH), :]
        w = ai[:, lanes(yy, CH)]
        add = jnp.dot(w, f, preferred_element_type=F32)
        yp[...] = add if first else yp[...] + add
        cov = lax.dot_general(ra[...], f, (((1,), (1,)), ((), ())), preferred_element_type=F32)
        cvf[:, lanes(yy, CH)] = cov
        cs[:, lanes(yy, CH)] = cov.astype(BF)

    def chunk_send(j):
        yy = y_from(j)
        for k in range(1, NX):
            send(
                cs.at[rows(xk[k], BR), lanes(yy, CH)], cr.at[k - 1, :, lanes(yy, CH)],
                cvs.at[k - 1, j], cvr.at[k - 1, j], dev(x_=xk[k]),
            )

    chunk(0, True)
    chunk_send(0)

    for k in Z_ORDER:
        arrived(plr.at[k - 1], plsr.at[k - 1])
    r, q = piece(l)
    acc = pa[r, q]
    for k in range(1, NL):
        acc = acc + plr[k - 1].astype(F32)
    done = acc.astype(BF)
    pq[...] = done

    def place(y_, l_):
        return (
            pl.ds(pl.multiple_of(y_ * 64 + lax.div(l_, 2) * 16, 16), 16),
            lanes(lax.rem(l_, 2), 384),
        )

    r, q = place(y, l)
    pf[r, q] = done
    for k in Z_ORDER:
        send(pq, pf.at[r, q], pfzs.at[k - 1], pfr.at[y * NL + l], dev(l_=lk[k]))
    for k in range(1, NY):
        send(pq, pf.at[r, q], pfys.at[0, k - 1], pfr.at[y * NL + l], dev(y_=yk[k]))

    for j in range(1, NY):
        yy = y_from(j)
        for b in range(NL):
            arrived(lhs.at[rows(yy * NL + b, BR)], lr.at[yy * NL + b])
        chunk(j, False)
        if j == NY - 1:
            half = rows(1 - c, 96)
            send(yp.at[half], yc, yss.at[0], ysr.at[0], dev(c_=1 - c))
        chunk_send(j)

    for k in Z_ORDER:
        i = l_from(k)
        r, q = place(y, i)
        arrived(pf.at[r, q], pfr.at[y * NL + i])
        for n in range(1, NY):
            send(pf.at[r, q], pf.at[r, q], pfys.at[k, n - 1], pfr.at[y * NL + i], dev(y_=yk[n]))

    arrived(yc, ysr.at[0])
    keep = rows(c, 96)
    ysum = yp[keep, :] + yc[...]
    yhs[...] = ysum.astype(BF)
    send(yhs, yhr, yss.at[1], ysr.at[1], dev(h_=1 - h))

    for k in range(1, NX):
        for j in range(NY):
            s = lanes(y_from(j), CH)
            arrived(cr.at[k - 1, :, s], cvr.at[k - 1, j])
    cov = cvf[rows(x, BR), :]
    for k in range(1, NX):
        cov = cov + cr[k - 1].astype(F32)
    out_f[...] = 0.2 * fac[...] + 0.8 * (cov * (1.0 / 1024.0))

    arrived(yhr, ysr.at[1])
    yb[keep, :] = (ysum + yhr[...].astype(F32)).astype(BF)
    send(yb.at[keep], yb.at[keep], yss.at[2], ysr.at[2], dev(c_=1 - c))

    for j in range(1, NY):
        for b in range(NL):
            r, q = place(yk[j], b)
            arrived(pf.at[r, q], pfr.at[yk[j] * NL + b])
    arrived(yb.at[rows(1 - c, 96)], ysr.at[2])

    res = jnp.dot(yb[...], pf[...], preferred_element_type=F32)
    mf[...] = res
    ms[...] = res.astype(BF)
    for k in range(1, NX):
        send(ms.at[rows(xk[k], BR)], mr.at[k - 1], mss.at[k - 1], msr.at[k - 1], dev(x_=xk[k]))
    acc = mf[rows(x, BR), :]
    for k in range(1, NX):
        arrived(mr.at[k - 1], msr.at[k - 1])
        acc = acc + mr[k - 1].astype(F32)
    out_m[...] = 0.9 * mom[...] + acc

    for near in t0:

        @pl.when(x != g)
        def _(near=near):
            near.wait_send()

    for cp in pending:
        cp.wait_send()


def shards(
    activations, output_grads, output_inverse, input_inverse, owner_table, factor_slab, momentum
):
    g = lax.axis_index("grad")
    owners = lax.dynamic_slice(owner_table, (g * 32,), (32,))
    ainv = input_inverse.reshape(BR, 128, BR)[:, owners, :].reshape(BR, SLAB)
    vm = pl.BlockSpec(memory_space=pltpu.VMEM)
    dma = pltpu.SemaphoreType.DMA
    new_momentum, factor_t = pl.pallas_call(
        kernel,
        out_shape=(
            jax.ShapeDtypeStruct((BR, CG), F32),
            jax.ShapeDtypeStruct((BR, SLAB), F32),
        ),
        in_specs=[vm, vm, vm, pl.BlockSpec(memory_space=pl.ANY), vm, vm],
        out_specs=(vm, vm),
        scratch_shapes=[
            pltpu.VMEM((192, TK), BF),
            pltpu.VMEM((192, TK), BF),
            pltpu.VMEM((SLAB, TK), BF),
            pltpu.VMEM((192, SLAB), BF),
            pltpu.VMEM((192, CG), BF),
            pltpu.VMEM((192, SLAB), F32),
            pltpu.VMEM((192, SLAB), BF),
            pltpu.VMEM((3, BR, SLAB), BF),
            pltpu.VMEM((192, TK), F32),
            pltpu.VMEM((96, TK), F32),
            pltpu.VMEM((96, TK), BF),
            pltpu.VMEM((96, TK), BF),
            pltpu.VMEM((192, TK), BF),
            pltpu.VMEM((TK, CG), F32),
            pltpu.VMEM((TK, CG), BF),
            pltpu.VMEM((3, 64, CG), BF),
            pltpu.VMEM((64, CG), F32),
            pltpu.VMEM((64, CG), BF),
            pltpu.VMEM((7, 16, 384), BF),
            pltpu.VMEM((16, 384), BF),
            pltpu.VMEM((TK, CG), BF),
            pltpu.VMEM((192, CG), F32),
            pltpu.VMEM((192, CG), BF),
            pltpu.VMEM((3, BR, CG), BF),
            dma((2,)), dma((2, 2)), dma((2, 2)), dma((2, 2)), dma((2, 2)),
            dma((7,)), dma((8, 3)), dma((32,)),
            dma((3,)), dma((3,)), dma((3,)), dma((3,)),
            dma((3, 4)), dma((3, 4)), dma((3,)), dma((3,)),
            dma((3,)), dma((3,)), dma((7,)), dma((7,)),
            dma((7,)), dma((8, 3)), dma((32,)), dma((3,)), dma((3,)),
        ],
        compiler_params=pltpu.CompilerParams(
            collective_id=0, has_side_effects=True, vmem_limit_bytes=32 << 20
        ),
        cost_estimate=pl.CostEstimate(
            flops=2 * 230_000_000, bytes_accessed=2_000_000, transcendentals=0
        ),
        name="kfac",
    )(activations.T, output_grads.T, ainv, output_inverse, factor_slab.T, momentum)
    return (new_momentum, factor_t.T)


def solution(mesh):
    return jax.shard_map(
        shards,
        mesh=mesh,
        in_specs=(
            P("grad", "dp"),
            P("grad", "dp"),
            P("dp", None),
            P("dp", None),
            P(),
            P("grad", "dp"),
            P("dp", "grad"),
        ),
        out_specs=(P("dp", "grad"), P("grad", "dp")),
        check_vma=False,
    )
```

time: 2180 us -> 77.5 us (0.04)
  the two profiles are of different devices: /device:TPU:256 before, /device:TPU:61 now
where the time goes in v1:
time: 77.5 us; the launch traced here: 77.4 us
  Pallas kernels  70.3 us (91%)
  local copies, waits for them, and re-layouts  6.22 us (8%)
    pallas_call x1, Pallas kernels, shards(): pl.pallas_call(kernel, out_shape=(jax.ShapeDtypeStruct((BR, CG), F32), ja...  70.3 us
    reshape x3, local copies, waits for them, and re-layouts, shards(): ainv = input_inverse.reshape(BR, 128, BR)[:, owners, :].reshape(BR, SLAB)  4.08 us

profile of v1, /device:TPU:61, one launch (start us, length us, event | category | flops | bytes accessed | tf_op | source)
XLA Modules:
  0.0 77.4 jit_solution(15025924472613567475)
XLA Ops:
  0.6 2.5 %reshape.10 = bf16[48,128,48]{2,1,0:T(8,128)(2,1)S(1)} reshape(bf16[48,6144]{1,0:T(8,128)(2,1)} %param.10) | data formatting | bytes 1179648 | tf_op jit(solution)/shard_map/reshape | solution.py:302
  3.2 0.0 copy-start.5
  3.2 1.0 %copy.9 = bf16[48,128,48]{2,0,1:T(8,128)(2,1)S(1)} copy(bf16[48,128,48]{2,1,0:T(8,128)(2,1)S(1)} %reshape.10) | data formatting | bytes 1179648 | tf_op jit(solution)/shard_map/reshape | solution.py:302
  4.2 0.0 copy-start
  4.2 0.0 copy-start.1
  4.2 0.0 copy-start.2
  4.2 0.0 copy-start.3
  4.2 0.0 copy-start.4
  4.3 0.0 copy-done.5
  4.3 0.1 compare_select_fusion
  4.4 0.6 gather_fusion
  5.0 0.1 copy.10
  5.1 0.5 reshape.11.ainv
  5.6 0.0 copy-done
  5.7 0.0 copy-done.1
  5.7 0.0 copy-done.2
  5.7 0.0 copy-done.3
  5.7 0.0 copy-done.4
  5.7 70.3 %kfac.1 = (f32[48,768]{1,0:T(8,128)S(1)}, f32[48,1536]{1,0:T(8,128)S(1)}) custom-call(bf16[48,256]{1,0:T(8,128)(2,1)S(1)} %bitcast.7, bf16[48,256]{1,0:T(8,128)(2,1)S(1)} %bitcast.8, bf16[48,1536]{1,0:T(8,128)(2,1)S(1)} %reshape.11.ainv, bf16[48,3072]{1,0:T(8,128)(2,1)S(1)} %copy-done, f32[48,1536]{1,0:T(8,128)S(1)} %bitcast.6, f32[48,768]{1,0:T(8,128)S(1)} %copy-done.2), custom_call_target="tpu_custom_call" | custom-call | flops 460000000 | bytes 2000000 | tf_op jit(solution)/shard_map/kfac/pallas_call | solution.py:305
  76.0 0.7 copy.13
  76.7 0.7 copy.14
  (1 shorter events, 0.0 us)
Async XLA Ops:
  3.2 1.1 %copy-start.5 = (s32[128]{0:T(128)S(1)}, s32[128]{0:T(128)}, u32[]{:S(2)}) copy-start(s32[128]{0:T(128)} %param.11) | copy-start | bytes 1540
  4.2 1.4 %copy-start = (bf16[48,3072]{1,0:T(8,128)(2,1)S(1)}, bf16[48,3072]{1,0:T(8,128)(2,1)}, u32[]{:S(2)}) copy-start(bf16[48,3072]{1,0:T(8,128)(2,1)} %oinv.1) | copy-start | bytes 884740
  4.2 1.4 %copy-start.1 = (f32[1536,48]{0,1:T(8,128)S(1)}, f32[1536,48]{0,1:T(8,128)}, u32[]{:S(2)}) copy-start(f32[1536,48]{0,1:T(8,128)} %param.12) | copy-start | bytes 884740
  4.2 1.4 %copy-start.2 = (f32[48,768]{1,0:T(8,128)S(1)}, f32[48,768]{1,0:T(8,128)}, u32[]{:S(2)}) copy-start(f32[48,768]{1,0:T(8,128)} %mom.1) | copy-start | bytes 442372
  4.2 1.4 %copy-start.3 = (bf16[256,48]{0,1:T(8,128)(2,1)S(1)}, bf16[256,48]{0,1:T(8,128)(2,1)}, u32[]{:S(2)}) copy-start(bf16[256,48]{0,1:T(8,128)(2,1)} %param.7) | copy-start | bytes 73732
  4.2 1.4 %copy-start.4 = (bf16[256,48]{0,1:T(8,128)(2,1)S(1)}, bf16[256,48]{0,1:T(8,128)(2,1)}, u32[]{:S(2)}) copy-start(bf16[256,48]{0,1:T(8,128)(2,1)} %param.8) | copy-start | bytes 73732

commit v2 on v1

v2 whole, which is shorter than its diff:
```python
import functools

import jax
import jax.numpy as jnp
from jax import lax
from jax.experimental import pallas as pl
from jax.experimental.pallas import tpu as pltpu
from jax.sharding import PartitionSpec as P

MESH = pl.DeviceIdType.MESH
BF = jnp.bfloat16
F32 = jnp.float32
NX, NY, NL = 4, 4, 8
BR = 48
TK = 256
SLAB = 1536
CH = NL * BR
CG = 768


def kernel(
    at, gt, ainv, oinv, owners, fac, mom, out_m, out_f,
    av, ow, fv, mv, ra, rg, lhs, an, ap, ai, oi, cvf, cs, cr, yp, yc, yhs, yhr, yb,
    pp, pys, pyr, pa, pls, plr, pb, pbs, plp, pq, pf, mf, ms, mr,
    loc, t0s, t0r, fws, fwr, zs, ys, lr, ais, air, ois, oir, cvs, cvr, yss, ysr,
    pyss, pysr, plss, plsr, pfzs, pfys, pfr, mss, msr,
):
    dp = lax.axis_index("dp")
    g = lax.axis_index("grad")
    x = lax.div(dp, 32)
    y = lax.rem(lax.div(dp, 8), 4)
    l = lax.rem(dp, 8)
    h = lax.div(g, 2)
    c = lax.rem(g, 2)

    def dev(x_=None, y_=None, l_=None, h_=None, c_=None):
        x_ = x if x_ is None else x_
        y_ = y if y_ is None else y_
        l_ = l if l_ is None else l_
        h_ = h if h_ is None else h_
        c_ = c if c_ is None else c_
        return ((x_ * NY + y_) * NL + l_, h_ * 2 + c_)

    def rows(i, n):
        return pl.ds(pl.multiple_of(i * n, 16), n)

    def lanes(i, n):
        return pl.ds(pl.multiple_of(i * n, 128), n)

    pending = []

    def send(src, dst, ss, rs, to):
        cp = pltpu.make_async_remote_copy(
            src_ref=src, dst_ref=dst, send_sem=ss, recv_sem=rs, device_id=to, device_id_type=MESH
        )
        cp.start()
        pending.append(cp)

    def arrived(dst, sem):
        pltpu.make_async_copy(dst, dst, sem).wait()

    xk = [lax.rem(x + k, NX) for k in range(NX)]
    yk = [lax.rem(y + k, NY) for k in range(NY)]
    quad = lax.div(l, 4)
    lp = lax.rem(l + 4, NL)
    lq = [quad * 4 + lax.rem(l + k, 4) for k in range(4)]

    def x_from(k):
        return lax.rem(x + (NX - k), NX)

    def y_from(k):
        return lax.rem(y + (NY - k), NY)

    def lq_from(k):
        return quad * 4 + lax.rem(l + (4 - k), 4)

    own = [
        pltpu.make_async_copy(owners, ow, loc.at[0]),
        pltpu.make_async_copy(ainv, av, loc.at[1]),
        pltpu.make_async_copy(oinv.at[:, lanes(g, CG)], oi.at[rows(x, BR)], loc.at[2]),
        pltpu.make_async_copy(mom, mv, loc.at[3]),
        pltpu.make_async_copy(fac, fv, loc.at[4]),
    ]
    for cp in own:
        cp.start()

    bar = pltpu.get_barrier_semaphore()

    def greet(to):
        pl.semaphore_signal(bar, inc=1, device_id=to, device_id_type=MESH)

    for j in range(2):
        x0 = c + 2 * j

        @pl.when(jnp.logical_or(x0 != x, x != g))
        def _():
            greet(dev(x_=x0, h_=lax.div(x, 2), c_=lax.rem(x, 2)))

    greet(dev(h_=1 - h))
    greet(dev(l_=lp))
    for k in range(1, NX):
        greet(dev(x_=xk[k]))
        greet(dev(y_=yk[k]))
        greet(dev(l_=lq[k]))
    greet(dev(c_=1 - c))

    own[1].wait()
    for j in range(16):
        an[pl.ds(j * CH, CH), 0:BR] = av[:, pl.ds(j * CH, CH)].astype(F32).T

    pl.semaphore_wait(bar, 14 - jnp.where(x == g, 1, 0))

    cc = lax.rem(x, 2)
    xj = lax.div(x, 2)

    def first(a, src, dst):
        there = pltpu.make_async_remote_copy(
            src_ref=src, dst_ref=dst.at[rows(x, BR)], send_sem=t0s.at[a, 0], recv_sem=t0r.at[a, xj],
            device_id=dev(x_=g, h_=xj, c_=cc), device_id_type=MESH,
        )
        here = pltpu.make_async_copy(src, dst.at[rows(x, BR)], t0r.at[a, xj])

        @pl.when(x != g)
        def _():
            there.start()

        @pl.when(x == g)
        def _():
            here.start()

        return there

    def second(a, src, dst):
        send(src, dst.at[rows(x, BR)], t0s.at[a, 1], t0r.at[a, xj], dev(x_=g, h_=1 - xj, c_=cc))

    t0 = [first(0, at, ra)]
    second(1, gt, rg)
    t0.append(first(1, gt, rg))
    r = rows(x, BR)
    own[2].wait()
    for k in range(1, NX):
        send(oi.at[r], oi.at[r], ois.at[k - 1], oir.at[k - 1], dev(x_=xk[k]))

    own[0].wait()
    natural = lax.broadcasted_iota(jnp.int32, (32, 128), 1)
    pick = jnp.where(ow[pl.ds(pl.multiple_of(g * 32, 8), 32), :] == natural, 1.0, 0.0).astype(BF)
    for j in range(BR):
        col = an[pl.ds(j, 128, stride=BR), :].astype(BF)
        ap[pl.ds(j, 32, stride=BR), :] = jnp.dot(pick, col, preferred_element_type=F32)

    blk = ra.at[rows(g, BR)]
    mine = rows(y * NL + l, BR)
    arrived(blk, t0r.at[0, h])
    send(blk, lhs.at[mine], zs.at[0], lr.at[y * NL + l], dev(l_=lp))
    for k in range(1, 4):
        send(blk, lhs.at[mine], zs.at[k], lr.at[y * NL + l], dev(l_=lq[k]))
    for k in range(1, NY):
        send(blk, lhs.at[mine], ys.at[0, k - 1], lr.at[y * NL + l], dev(y_=yk[k]))
    lhs[mine, :] = ra[rows(g, BR), :]
    send(blk, blk, fws.at[0, 0], fwr.at[0, h], dev(c_=1 - c))

    for j in range(2):
        b = rg.at[rows(c + 2 * j, BR)]
        arrived(b, t0r.at[1, j])
        send(b, b, fws.at[1, j], fwr.at[1, j], dev(c_=1 - c))
    for j in range(2):
        arrived(rg.at[rows(1 - c + 2 * j, BR)], fwr.at[1, j])
    for k in range(1, NX):
        arrived(oi.at[rows(x_from(k), BR)], oir.at[k - 1])
    gm = rg[...].astype(F32).T.astype(BF)
    part = jnp.dot(gm, oi[...], preferred_element_type=F32)
    pp[...] = part
    pys[...] = part.astype(BF)
    for k in range(1, NY):
        send(pys.at[rows(yk[k], 64)], pyr.at[k - 1], pyss.at[k - 1], pysr.at[k - 1], dev(y_=yk[k]))

    def to_y(i, n):
        s = lhs.at[rows(i, BR)]
        for q in range(1, NY):
            send(s, s, ys.at[n, q - 1], lr.at[i], dev(y_=yk[q]))

    i = y * NL + lp
    s = lhs.at[rows(i, BR)]
    arrived(s, lr.at[i])
    for k in range(1, 4):
        send(s, s, zs.at[3 + k], lr.at[i], dev(l_=lq[k]))
    to_y(i, 1)
    for k in (1, 3, 2):
        i = y * NL + lq_from(k)
        arrived(lhs.at[rows(i, BR)], lr.at[i])
        to_y(i, 1 + k)

    for j in range(NY):
        ai[r, pl.ds(j * CH, CH)] = ap[pl.ds(j * CH, CH), 0:BR].T.astype(BF)
    for k in range(1, NX):
        send(ai.at[r], ai.at[r], ais.at[k - 1], air.at[k - 1], dev(x_=xk[k]))
    second(0, at, ra)

    for k in range(1, NY):
        arrived(pyr.at[k - 1], pysr.at[k - 1])
    acc = pp[rows(y, 64), :]
    for k in range(1, NY):
        acc = acc + pyr[k - 1].astype(F32)
    pa[...] = acc
    pls[...] = acc.astype(BF)
    for k in (1, 3, 2):
        b = rows(lax.rem(lq[k], 4), 16)
        send(pls.at[b], plr.at[k - 1], plss.at[k - 1], plsr.at[k - 1], dev(l_=lq[k]))

    for k in (1, 3, 2):
        i = y * NL + lax.rem(lq_from(k) + 4, NL)
        arrived(lhs.at[rows(i, BR)], lr.at[i])
        to_y(i, 4 + k)

    for k in (1, 3, 2):
        arrived(plr.at[k - 1], plsr.at[k - 1])
    acc = pa[rows(lax.rem(l, 4), 16), :]
    for k in range(1, 4):
        acc = acc + plr[k - 1].astype(F32)
    pb[...] = acc
    pbs[...] = acc.astype(BF)
    send(pbs.at[:, lanes(1 - quad, 384)], plp, plss.at[3], plsr.at[3], dev(l_=lp))

    for k in range(1, NX):
        arrived(ai.at[rows(x_from(k), BR)], air.at[k - 1])

    def y_part(j):
        f = lhs[rows(y_from(j), CH), :]
        w = ai[:, lanes(y_from(j), CH)]
        add = jnp.dot(w, f, preferred_element_type=F32)
        yp[...] = add if j == 0 else yp[...] + add

    y_part(0)

    arrived(plp, plsr.at[3])
    done = (pb[:, lanes(quad, 384)] + plp[...].astype(F32)).astype(BF)
    pq[...] = done

    def place(y_, l_):
        return (
            pl.ds(pl.multiple_of(y_ * 64 + lax.rem(l_, 4) * 16, 16), 16),
            lanes(lax.div(l_, 4), 384),
        )

    r, q = place(y, l)
    pf[r, q] = done
    send(pq, pf.at[r, q], pfzs.at[0], pfr.at[y * NL + l], dev(l_=lp))
    for k in range(1, 4):
        send(pq, pf.at[r, q], pfzs.at[k], pfr.at[y * NL + l], dev(l_=lq[k]))
    for k in range(1, NY):
        send(pq, pf.at[r, q], pfys.at[0, k - 1], pfr.at[y * NL + l], dev(y_=yk[k]))

    for j in range(1, NY):
        yy = y_from(j)
        for b in range(NL):
            arrived(lhs.at[rows(yy * NL + b, BR)], lr.at[yy * NL + b])
        y_part(j)
    send(yp.at[rows(1 - c, 96)], yc, yss.at[0], ysr.at[0], dev(c_=1 - c))

    def pf_to_y(i, n):
        r, q = place(y, i)
        for m in range(1, NY):
            send(pf.at[r, q], pf.at[r, q], pfys.at[n, m - 1], pfr.at[y * NL + i], dev(y_=yk[m]))

    r, q = place(y, lp)
    arrived(pf.at[r, q], pfr.at[y * NL + lp])
    for k in range(1, 4):
        send(pf.at[r, q], pf.at[r, q], pfzs.at[3 + k], pfr.at[y * NL + lp], dev(l_=lq[k]))
    pf_to_y(lp, 1)

    arrived(yc, ysr.at[0])
    keep = rows(c, 96)
    ysum = yp[keep, :] + yc[...]
    yhs[...] = ysum.astype(BF)
    send(yhs, yhr, yss.at[1], ysr.at[1], dev(h_=1 - h))

    for k in (1, 3, 2):
        i = lq_from(k)
        r, q = place(y, i)
        arrived(pf.at[r, q], pfr.at[y * NL + i])
        pf_to_y(i, 1 + k)
    for k in (1, 3, 2):
        i = lax.rem(lq_from(k) + 4, NL)
        r, q = place(y, i)
        arrived(pf.at[r, q], pfr.at[y * NL + i])
        pf_to_y(i, 4 + k)

    other = ra.at[rows(c + 2 * (1 - h), BR)]
    arrived(other, t0r.at[0, 1 - h])
    send(other, other, fws.at[0, 1], fwr.at[0, 1 - h], dev(c_=1 - c))
    for j in range(2):
        arrived(ra.at[rows(1 - c + 2 * j, BR)], fwr.at[0, j])
    for j in range(NY):
        s = lanes(y_from(j), CH)
        f = lhs[rows(y_from(j), CH), :]
        cov = lax.dot_general(ra[...], f, (((1,), (1,)), ((), ())), preferred_element_type=F32)
        cvf[:, s] = cov
        cs[:, s] = cov.astype(BF)
        for k in range(1, NX):
            send(
                cs.at[rows(xk[k], BR), s], cr.at[k - 1, :, s],
                cvs.at[k - 1, j], cvr.at[k - 1, j], dev(x_=xk[k]),
            )

    arrived(yhr, ysr.at[1])
    yb[keep, :] = (ysum + yhr[...].astype(F32)).astype(BF)
    send(yb.at[keep], yb.at[keep], yss.at[2], ysr.at[2], dev(c_=1 - c))

    for j in range(1, NY):
        for b in range(NL):
            r, q = place(yk[j], b)
            arrived(pf.at[r, q], pfr.at[yk[j] * NL + b])
    arrived(yb.at[rows(1 - c, 96)], ysr.at[2])

    for k in range(1, NX):
        b = rows(xk[k], BR)
        ms[b, :] = jnp.dot(yb[b, :], pf[...], preferred_element_type=F32).astype(BF)
        send(ms.at[b], mr.at[k - 1], mss.at[k - 1], msr.at[k - 1], dev(x_=xk[k]))
    own[3].wait()
    mf[...] = 0.9 * mv[...] + jnp.dot(yb[rows(x, BR), :], pf[...], preferred_element_type=F32)

    for k in range(1, NX):
        for j in range(NY):
            s = lanes(y_from(j), CH)
            arrived(cr.at[k - 1, :, s], cvr.at[k - 1, j])
    own[4].wait()
    cov = cvf[rows(x, BR), :]
    for k in range(1, NX):
        cov = cov + cr[k - 1].astype(F32)
    out_f[...] = 0.2 * fv[...] + 0.8 * (cov * (1.0 / 1024.0))

    acc = mf[...]
    for k in range(1, NX):
        arrived(mr.at[k - 1], msr.at[k - 1])
        acc = acc + mr[k - 1].astype(F32)
    out_m[...] = acc

    for there in t0:

        @pl.when(x != g)
        def _(there=there):
            there.wait_send()

    for cp in pending:
        cp.wait_send()


def shards(
    activations, output_grads, output_inverse, input_inverse, owner_table, factor_slab, momentum
):
    vm = pl.BlockSpec(memory_space=pltpu.VMEM)
    dma = pltpu.SemaphoreType.DMA
    new_momentum, factor_t = pl.pallas_call(
        kernel,
        out_shape=(
            jax.ShapeDtypeStruct((BR, CG), F32),
            jax.ShapeDtypeStruct((BR, SLAB), F32),
        ),
        in_specs=[pl.BlockSpec(memory_space=pl.ANY)] * 7,
        out_specs=(vm, vm),
        scratch_shapes=[
            pltpu.VMEM((BR, 128 * BR), BF),
            pltpu.VMEM((128, 1), jnp.int32),
            pltpu.VMEM((BR, SLAB), F32),
            pltpu.VMEM((BR, CG), F32),
            pltpu.VMEM((192, TK), BF),
            pltpu.VMEM((192, TK), BF),
            pltpu.VMEM((SLAB, TK), BF),
            pltpu.VMEM((128 * BR, 128), F32),
            pltpu.VMEM((SLAB, 128), F32),
            pltpu.VMEM((192, SLAB), BF),
            pltpu.VMEM((192, CG), BF),
            pltpu.VMEM((192, SLAB), F32),
            pltpu.VMEM((192, SLAB), BF),
            pltpu.VMEM((3, BR, SLAB), BF),
            pltpu.VMEM((192, TK), F32),
            pltpu.VMEM((96, TK), F32),
            pltpu.VMEM((96, TK), BF),
            pltpu.VMEM((96, TK), BF),
            pltpu.VMEM((192, TK), BF),
            pltpu.VMEM((TK, CG), F32),
            pltpu.VMEM((TK, CG), BF),
            pltpu.VMEM((3, 64, CG), BF),
            pltpu.VMEM((64, CG), F32),
            pltpu.VMEM((64, CG), BF),
            pltpu.VMEM((3, 16, CG), BF),
            pltpu.VMEM((16, CG), F32),
            pltpu.VMEM((16, CG), BF),
            pltpu.VMEM((16, 384), BF),
            pltpu.VMEM((16, 384), BF),
            pltpu.VMEM((TK, CG), BF),
            pltpu.VMEM((BR, CG), F32),
            pltpu.VMEM((192, CG), BF),
            pltpu.VMEM((3, BR, CG), BF),
            dma((5,)), dma((2, 2)), dma((2, 2)), dma((2, 2)), dma((2, 2)),
            dma((7,)), dma((8, 3)), dma((32,)),
            dma((3,)), dma((3,)), dma((3,)), dma((3,)),
            dma((3, 4)), dma((3, 4)), dma((3,)), dma((3,)),
            dma((3,)), dma((3,)), dma((4,)), dma((4,)),
            dma((7,)), dma((8, 3)), dma((32,)), dma((3,)), dma((3,)),
        ],
        compiler_params=pltpu.CompilerParams(
            collective_id=0, has_side_effects=True, vmem_limit_bytes=56 << 20
        ),
        cost_estimate=pl.CostEstimate(
            flops=2 * 230_000_000, bytes_accessed=2_000_000, transcendentals=0
        ),
        name="kfac",
    )(
        activations.T, output_grads.T, input_inverse, output_inverse, owner_table[:, None], factor_slab.T, momentum
    )
    return (new_momentum, factor_t.T)


def solution(mesh):
    return jax.shard_map(
        shards,
        mesh=mesh,
        in_specs=(
            P("grad", "dp"),
            P("grad", "dp"),
            P("dp", None),
            P("dp", None),
            P(),
            P("grad", "dp"),
            P("dp", "grad"),
        ),
        out_specs=(P("dp", "grad"), P("grad", "dp")),
        check_vma=False,
    )
```

time: 77.5 us -> 71.5 us (0.923)
  the two profiles are of different devices: /device:TPU:61 before, /device:TPU:1 now
where the time goes in v2:
time: 71.5 us; the launch traced here: 71.3 us
  Pallas kernels  66.9 us (94%)
  local copies, waits for them, and re-layouts  3.73 us (5%)
    pallas_call x1, Pallas kernels, shards(): pl.pallas_call(kernel, out_shape=(jax.ShapeDtypeStruct((BR, CG), F32), ja...  66.9 us
    unnamed x6, local copies, waits for them, and re-layouts  2.99 us

profile of v2, /device:TPU:1, one launch (start us, length us, event | category | flops | bytes accessed | tf_op | source)
XLA Modules:
  0.0 71.3 jit_solution(13067367242881816045)
XLA Ops:
  0.6 0.0 copy-start.1
  0.6 0.6 copy-done.1
  1.3 0.7 %copy.9.owners = s32[128,1]{1,0:T(8,128)} copy(s32[128,1]{0,1:T(1,128)S(1)} %bitcast.6) | data formatting | bytes 1024 | tf_op jit(solution)/shard_map/broadcast_in_dim | solution.py:410
  2.0 66.9 %kfac.1 = (f32[48,768]{1,0:T(8,128)}, f32[48,1536]{1,0:T(8,128)}) custom-call(bf16[48,256]{1,0:T(8,128)(2,1)} %bitcast.8, bf16[48,256]{1,0:T(8,128)(2,1)} %bitcast.9, bf16[48,6144]{1,0:T(8,128)(2,1)} %ainv.1, bf16[48,3072]{1,0:T(8,128)(2,1)} %oinv.1, s32[128,1]{1,0:T(8,128)} %copy.9.owners, f32[48,1536]{1,0:T(8,128)} %bitcast.7, f32[48,768]{1,0:T(8,128)} %mom.1), custom_call_target="tpu_custom_call" | custom-call | flops 460000000 | bytes 2000000 | tf_op jit(solution)/shard_map/kfac/pallas_call | solution.py:353
  68.9 0.0 copy-start
  68.9 1.6 %copy.12 = f32[48,768]{1,0:T(8,128)} copy(f32[48,768]{1,0:T(8,128)} %get-tuple-element.8) | data formatting | bytes 294912
  70.6 0.0 copy-done
  70.6 0.7 %copy.13 = f32[1536,48]{0,1:T(8,128)} copy(f32[1536,48]{0,1:T(8,128)S(1)} %bitcast.5) | data formatting | bytes 589824
Async XLA Ops:
  0.6 0.7 copy-start.1
  68.9 1.6 %copy-start = (f32[48,1536]{1,0:T(8,128)S(1)}, f32[48,1536]{1,0:T(8,128)}, u32[]{:S(2)}) copy-start(f32[48,1536]{1,0:T(8,128)} %get-tuple-element.5) | copy-start | bytes 884740

commit v3 on v2

v3 whole, which is shorter than its diff:
```python
import functools

import jax
import jax.numpy as jnp
from jax import lax
from jax.experimental import pallas as pl
from jax.experimental.pallas import tpu as pltpu
from jax.sharding import PartitionSpec as P

MESH = pl.DeviceIdType.MESH
BF = jnp.bfloat16
F32 = jnp.float32
NX, NY, NL = 4, 4, 8
BR = 48
TK = 256
SLAB = 1536
CH = NL * BR
CG = 768


def kernel(
    at, gt, ainv, oinv, owners, fac, mom, out_m, out_f,
    av, ow, fv, mv, ra, rg, lhs, an, ap, asb, ai, oi, cvf, cs, crc, cg, cfin, yp, ysb, yr, yb,
    pp, pys, pyr, pa, pls, plr, pb, pbs, plp, pq, pf, mo, mr, mf, ms, fin,
    loc, gs, gr, ars, arr, zs, ys, lr, ais, air, ois, oir, ccs, ccr, cfs, cfr,
    yss, ysr, yas, yar, pyss, pysr, plss, plsr, pfzs, pfys, pfr, mcs, mcr, mfs, mfr,
):
    dp = lax.axis_index("dp")
    g = lax.axis_index("grad")
    x = lax.div(dp, 32)
    y = lax.rem(lax.div(dp, 8), 4)
    l = lax.rem(dp, 8)
    h = lax.div(g, 2)
    c = lax.rem(g, 2)

    def dev(x_=None, y_=None, l_=None, h_=None, c_=None):
        x_ = x if x_ is None else x_
        y_ = y if y_ is None else y_
        l_ = l if l_ is None else l_
        h_ = h if h_ is None else h_
        c_ = c if c_ is None else c_
        return ((x_ * NY + y_) * NL + l_, h_ * 2 + c_)

    def rows(i, n):
        return pl.ds(pl.multiple_of(i * n, 16), n)

    def lanes(i, n):
        return pl.ds(pl.multiple_of(i * n, 128), n)

    pending = []

    def send(src, dst, ss, rs, to):
        cp = pltpu.make_async_remote_copy(
            src_ref=src, dst_ref=dst, send_sem=ss, recv_sem=rs, device_id=to, device_id_type=MESH
        )
        cp.start()
        pending.append(cp)

    def arrived(dst, sem):
        pltpu.make_async_copy(dst, dst, sem).wait()

    xk = [lax.rem(x + k, NX) for k in range(NX)]
    yk = [lax.rem(y + k, NY) for k in range(NY)]
    quad = lax.div(l, 4)
    lp = lax.rem(l + 4, NL)
    lq = [quad * 4 + lax.rem(l + k, 4) for k in range(4)]

    def x_from(k):
        return lax.rem(x + (NX - k), NX)

    def y_from(k):
        return lax.rem(y + (NY - k), NY)

    def lq_from(k):
        return quad * 4 + lax.rem(l + (4 - k), 4)

    mine = rows(y * NL + l, BR)
    r = rows(x, BR)
    own = [
        pltpu.make_async_copy(owners, ow, loc.at[0]),
        pltpu.make_async_copy(ainv, av, loc.at[1]),
        pltpu.make_async_copy(oinv.at[:, lanes(x, CG)], oi.at[r], loc.at[2]),
        pltpu.make_async_copy(gt, rg.at[r], loc.at[3]),
        pltpu.make_async_copy(at, ra.at[r], loc.at[4]),
        pltpu.make_async_copy(at, lhs.at[mine], loc.at[5]),
        pltpu.make_async_copy(mom, mv, loc.at[6]),
        pltpu.make_async_copy(fac, fv, loc.at[7]),
    ]
    for cp in own:
        cp.start()

    bar = pltpu.get_barrier_semaphore()

    def greet(to):
        pl.semaphore_signal(bar, inc=1, device_id=to, device_id_type=MESH)

    for j in range(2):

        @pl.when(jnp.logical_or(h != j, x != g))
        def _():
            greet(dev(x_=g, h_=j, c_=lax.rem(x, 2)))

    greet(dev(l_=lp))
    for k in range(1, NX):
        greet(dev(x_=xk[k]))
        greet(dev(y_=yk[k]))
        greet(dev(l_=lq[k]))
    greet(dev(c_=1 - c))

    own[1].wait()
    for j in range(16):
        an[pl.ds(j * CH, CH), 0:BR] = av[:, pl.ds(j * CH, CH)].astype(F32).T
    own[0].wait()

    pl.semaphore_wait(bar, 13 - jnp.where(x == g, 1, 0))

    send(at, lhs.at[mine], zs.at[0], lr.at[y * NL + l], dev(l_=lp))
    for k in range(1, NX):
        send(gt, rg.at[r], gs.at[k - 1], gr.at[k - 1], dev(x_=xk[k]))
    for k in range(1, 4):
        send(at, lhs.at[mine], zs.at[k], lr.at[y * NL + l], dev(l_=lq[k]))
    for k in range(1, NX):
        send(oinv.at[:, lanes(xk[k], CG)], oi.at[r], ois.at[k - 1], oir.at[k - 1], dev(x_=xk[k]))
    for k in range(1, NY):
        send(at, lhs.at[mine], ys.at[0, k - 1], lr.at[y * NL + l], dev(y_=yk[k]))

    natural = lax.broadcasted_iota(jnp.int32, (128, 128), 1)
    pick = jnp.where(ow[...] == natural, 1.0, 0.0).astype(BF)
    for j in range(BR):
        col = an[pl.ds(j, 128, stride=BR), :].astype(BF)
        ap[pl.ds(j, 128, stride=BR), :] = jnp.dot(pick, col, preferred_element_type=F32)

    def to_y(i, n):
        s = lhs.at[rows(i, BR)]
        for q in range(1, NY):
            send(s, s, ys.at[n, q - 1], lr.at[i], dev(y_=yk[q]))

    i = y * NL + lp
    s = lhs.at[rows(i, BR)]
    arrived(s, lr.at[i])
    for k in range(1, 4):
        send(s, s, zs.at[3 + k], lr.at[i], dev(l_=lq[k]))
    to_y(i, 1)
    own[2].wait()
    own[3].wait()
    for k in range(1, NX):
        arrived(rg.at[rows(x_from(k), BR)], gr.at[k - 1])
    for k in range(1, NX):
        arrived(oi.at[rows(x_from(k), BR)], oir.at[k - 1])
    gm = rg[...].astype(F32).T.astype(BF)
    part = jnp.dot(gm, oi[...], preferred_element_type=F32)
    pp[...] = part
    pys[...] = part.astype(BF)
    for k in range(1, NY):
        send(pys.at[rows(yk[k], 64)], pyr.at[k - 1], pyss.at[k - 1], pysr.at[k - 1], dev(y_=yk[k]))

    for k in (1, 3, 2):
        i = y * NL + lq_from(k)
        arrived(lhs.at[rows(i, BR)], lr.at[i])
        to_y(i, 1 + k)

    for j in range(16):
        asb[:, pl.ds(j * CH, CH)] = ap[pl.ds(j * CH, CH), 0:BR].T.astype(BF)
    for k in range(1, NX):
        send(asb.at[:, lanes(xk[k], SLAB)], ai.at[r], ais.at[k - 1], air.at[k - 1], dev(x_=xk[k]))
    keep = pltpu.make_async_copy(asb.at[:, lanes(x, SLAB)], ai.at[r], loc.at[8])
    keep.start()
    for k in range(1, NX):
        send(at, ra.at[r], ars.at[k - 1], arr.at[k - 1], dev(x_=xk[k]))

    for k in range(1, NY):
        arrived(pyr.at[k - 1], pysr.at[k - 1])
    acc = pp[rows(y, 64), :]
    for k in range(1, NY):
        acc = acc + pyr[k - 1].astype(F32)
    pa[...] = acc
    pls[...] = acc.astype(BF)
    for k in (1, 3, 2):
        b = rows(lax.rem(lq[k], 4), 16)
        send(pls.at[b], plr.at[k - 1], plss.at[k - 1], plsr.at[k - 1], dev(l_=lq[k]))

    for k in (1, 3, 2):
        i = y * NL + lax.rem(lq_from(k) + 4, NL)
        arrived(lhs.at[rows(i, BR)], lr.at[i])
        to_y(i, 4 + k)

    for k in (1, 3, 2):
        arrived(plr.at[k - 1], plsr.at[k - 1])
    acc = pa[rows(lax.rem(l, 4), 16), :]
    for k in range(1, 4):
        acc = acc + plr[k - 1].astype(F32)
    pb[...] = acc
    pbs[...] = acc.astype(BF)
    send(pbs.at[:, lanes(1 - quad, 384)], plp, plss.at[3], plsr.at[3], dev(l_=lp))

    own[5].wait()
    keep.wait()
    for k in range(1, NX):
        arrived(ai.at[rows(x_from(k), BR)], air.at[k - 1])

    def y_part(j):
        f = lhs[rows(y_from(j), CH), :]
        w = ai[:, lanes(y_from(j), CH)]
        add = jnp.dot(w, f, preferred_element_type=F32)
        yp[...] = add if j == 0 else yp[...] + add

    y_part(0)

    arrived(plp, plsr.at[3])
    done = (pb[:, lanes(quad, 384)] + plp[...].astype(F32)).astype(BF)
    pq[...] = done

    def place(y_, l_):
        return (
            pl.ds(pl.multiple_of(y_ * 64 + lax.rem(l_, 4) * 16, 16), 16),
            lanes(lax.div(l_, 4), 384),
        )

    r, q = place(y, l)
    pf[r, q] = done
    send(pq, pf.at[r, q], pfzs.at[0], pfr.at[y * NL + l], dev(l_=lp))
    for k in range(1, 4):
        send(pq, pf.at[r, q], pfzs.at[k], pfr.at[y * NL + l], dev(l_=lq[k]))
    for k in range(1, NY):
        send(pq, pf.at[r, q], pfys.at[0, k - 1], pfr.at[y * NL + l], dev(y_=yk[k]))

    for j in range(1, NY):
        yy = y_from(j)
        for b in range(NL):
            arrived(lhs.at[rows(yy * NL + b, BR)], lr.at[yy * NL + b])
        y_part(j)

    ysb[...] = yp[...].astype(BF)
    for k in range(1, NX):
        send(ysb.at[rows(xk[k], BR)], yr.at[k - 1], yss.at[k - 1], ysr.at[k - 1], dev(x_=xk[k]))

    def pf_to_y(i, n):
        r, q = place(y, i)
        for m in range(1, NY):
            send(pf.at[r, q], pf.at[r, q], pfys.at[n, m - 1], pfr.at[y * NL + i], dev(y_=yk[m]))

    r, q = place(y, lp)
    arrived(pf.at[r, q], pfr.at[y * NL + lp])
    for k in range(1, 4):
        send(pf.at[r, q], pf.at[r, q], pfzs.at[3 + k], pfr.at[y * NL + lp], dev(l_=lq[k]))
    pf_to_y(lp, 1)

    for k in range(1, NX):
        arrived(yr.at[k - 1], ysr.at[k - 1])
    acc = yp[rows(x, BR), :]
    for k in range(1, NX):
        acc = acc + yr[k - 1].astype(F32)
    r = rows(x, BR)
    yb[r, :] = acc.astype(BF)
    for k in range(1, NX):
        send(yb.at[r], yb.at[r], yas.at[k - 1], yar.at[k - 1], dev(x_=xk[k]))

    for k in (1, 3, 2):
        i = lq_from(k)
        r, q = place(y, i)
        arrived(pf.at[r, q], pfr.at[y * NL + i])
        pf_to_y(i, 1 + k)
    for k in (1, 3, 2):
        i = lax.rem(lq_from(k) + 4, NL)
        r, q = place(y, i)
        arrived(pf.at[r, q], pfr.at[y * NL + i])
        pf_to_y(i, 4 + k)

    own[4].wait()
    for k in range(1, NX):
        arrived(ra.at[rows(x_from(k), BR)], arr.at[k - 1])
    for j in range(NY):
        s = lanes(y_from(j), CH)
        f = lhs[rows(y_from(j), CH), :]
        cov = lax.dot_general(ra[...], f, (((1,), (1,)), ((), ())), preferred_element_type=F32)
        cvf[:, s] = cov
        cs[:, s] = cov.astype(BF)
        for b in range(2):
            send(
                cs.at[rows(1 - c + 2 * b, BR), s], crc.at[b, :, s],
                ccs.at[b, j], ccr.at[b, j], dev(c_=1 - c),
            )

    parted = []

    def to_owner(src, dst, ss, rs, b):
        there = pltpu.make_async_remote_copy(
            src_ref=src, dst_ref=dst, send_sem=ss, recv_sem=rs,
            device_id=dev(x_=c + 2 * b, h_=lax.div(x, 2), c_=lax.rem(x, 2)), device_id_type=MESH,
        )
        here = pltpu.make_async_copy(src, dst, rs)
        is_own = jnp.logical_and(x == g, h == b)

        @pl.when(jnp.logical_not(is_own))
        def _():
            there.start()

        @pl.when(is_own)
        def _():
            here.start()

        parted.append((there, is_own))

    def cov_to_owner():
        for j in range(NY):
            s = lanes(y_from(j), CH)
            for b in range(2):
                arrived(crc.at[b, :, s], ccr.at[b, j])
                cg[b, :, s] = (cvf[rows(c + 2 * b, BR), s] + crc[b, :, s].astype(F32)).astype(BF)
                to_owner(cg.at[b, :, s], cfin.at[h, :, s], cfs.at[b, j], cfr.at[h, j], b)

    cov_to_owner()

    for j in range(1, NY):
        for b in range(NL):
            r, q = place(yk[j], b)
            arrived(pf.at[r, q], pfr.at[yk[j] * NL + b])
    for k in range(1, NX):
        arrived(yb.at[rows(x_from(k), BR)], yar.at[k - 1])

    for b in range(2):
        mo[b] = jnp.dot(yb[rows(1 - c + 2 * b, BR), :], pf[...], preferred_element_type=F32)
        send(mo.at[b], mr.at[b], mcs.at[b], mcr.at[b], dev(c_=1 - c))
    for b in range(2):
        mf[b] = jnp.dot(yb[rows(c + 2 * b, BR), :], pf[...], preferred_element_type=F32)
    for b in range(2):
        arrived(mr.at[b], mcr.at[b])
        ms[b] = (mf[b] + mr[b]).astype(BF)
        to_owner(ms.at[b], fin.at[h], mfs.at[b], mfr.at[h], b)

    own[7].wait()
    for k in range(2):
        for j in range(NY):
            s = lanes(y_from(j), CH)
            arrived(cfin.at[k, :, s], cfr.at[k, j])
    cov = cfin[0].astype(F32) + cfin[1].astype(F32)
    out_f[...] = 0.2 * fv[...] + 0.8 * (cov * (1.0 / 1024.0))

    own[6].wait()
    for k in range(2):
        arrived(fin.at[k], mfr.at[k])
    out_m[...] = 0.9 * mv[...] + (fin[0].astype(F32) + fin[1].astype(F32))

    for there, is_own in parted:

        @pl.when(jnp.logical_not(is_own))
        def _(there=there):
            there.wait_send()

    for cp in pending:
        cp.wait_send()


def shards(
    activations, output_grads, output_inverse, input_inverse, owner_table, factor_slab, momentum
):
    vm = pl.BlockSpec(memory_space=pltpu.VMEM)
    dma = pltpu.SemaphoreType.DMA
    new_momentum, factor_t = pl.pallas_call(
        kernel,
        out_shape=(
            jax.ShapeDtypeStruct((BR, CG), F32),
            jax.ShapeDtypeStruct((BR, SLAB), F32),
        ),
        in_specs=[pl.BlockSpec(memory_space=pl.ANY)] * 7,
        out_specs=(vm, vm),
        scratch_shapes=[
            pltpu.VMEM((BR, 128 * BR), BF),
            pltpu.VMEM((128, 1), jnp.int32),
            pltpu.VMEM((BR, SLAB), F32),
            pltpu.VMEM((BR, CG), F32),
            pltpu.VMEM((192, TK), BF),
            pltpu.VMEM((192, TK), BF),
            pltpu.VMEM((SLAB, TK), BF),
            pltpu.VMEM((128 * BR, 128), F32),
            pltpu.VMEM((128 * BR, 128), F32),
            pltpu.VMEM((BR, 128 * BR), BF),
            pltpu.VMEM((192, SLAB), BF),
            pltpu.VMEM((192, CG), BF),
            pltpu.VMEM((192, SLAB), F32),
            pltpu.VMEM((192, SLAB), BF),
            pltpu.VMEM((2, BR, SLAB), BF),
            pltpu.VMEM((2, BR, SLAB), BF),
            pltpu.VMEM((2, BR, SLAB), BF),
            pltpu.VMEM((192, TK), F32),
            pltpu.VMEM((192, TK), BF),
            pltpu.VMEM((3, BR, TK), BF),
            pltpu.VMEM((192, TK), BF),
            pltpu.VMEM((TK, CG), F32),
            pltpu.VMEM((TK, CG), BF),
            pltpu.VMEM((3, 64, CG), BF),
            pltpu.VMEM((64, CG), F32),
            pltpu.VMEM((64, CG), BF),
            pltpu.VMEM((3, 16, CG), BF),
            pltpu.VMEM((16, CG), F32),
            pltpu.VMEM((16, CG), BF),
            pltpu.VMEM((16, 384), BF),
            pltpu.VMEM((16, 384), BF),
            pltpu.VMEM((TK, CG), BF),
            pltpu.VMEM((2, BR, CG), F32),
            pltpu.VMEM((2, BR, CG), F32),
            pltpu.VMEM((2, BR, CG), F32),
            pltpu.VMEM((2, BR, CG), BF),
            pltpu.VMEM((2, BR, CG), BF),
            dma((9,)),
            dma((3,)),
            dma((3,)),
            dma((3,)),
            dma((3,)),
            dma((7,)),
            dma((8, 3)),
            dma((32,)),
            dma((3,)),
            dma((3,)),
            dma((3,)),
            dma((3,)),
            dma((2, 4)),
            dma((2, 4)),
            dma((2, 4)),
            dma((2, 4)),
            dma((3,)),
            dma((3,)),
            dma((3,)),
            dma((3,)),
            dma((3,)),
            dma((3,)),
            dma((4,)),
            dma((4,)),
            dma((7,)),
            dma((8, 3)),
            dma((32,)),
            dma((2,)),
            dma((2,)),
            dma((2,)),
            dma((2,)),
        ],
        compiler_params=pltpu.CompilerParams(
            collective_id=0, has_side_effects=True, vmem_limit_bytes=56 << 20
        ),
        cost_estimate=pl.CostEstimate(
            flops=2 * 230_000_000, bytes_accessed=2_000_000, transcendentals=0
        ),
        name="kfac",
    )(
        activations.T, output_grads.T, input_inverse, output_inverse, owner_table[:, None], factor_slab.T, momentum
    )
    return (new_momentum, factor_t.T)


def solution(mesh):
    return jax.shard_map(
        shards,
        mesh=mesh,
        in_specs=(
            P("grad", "dp"),
            P("grad", "dp"),
            P("dp", None),
            P("dp", None),
            P(),
            P("grad", "dp"),
            P("dp", "grad"),
        ),
        out_specs=(P("dp", "grad"), P("grad", "dp")),
        check_vma=False,
    )
```

time: 71.5 us -> 99.4 us (1.39)
  the two profiles are of different devices: /device:TPU:1 before, /device:TPU:36 now
where the time goes in v3:
time: 99.4 us; the launch traced here: 99.2 us
  Pallas kernels  94.8 us (95%)
  local copies, waits for them, and re-layouts  3.73 us (4%)
    pallas_call x1, Pallas kernels, shards(): pl.pallas_call(kernel, out_shape=(jax.ShapeDtypeStruct((BR, CG), F32), ja...  94.8 us
    unnamed x6, local copies, waits for them, and re-layouts  2.99 us

profile of v3, /device:TPU:36, one launch (start us, length us, event | category | flops | bytes accessed | tf_op | source)
XLA Modules:
  0.0 99.2 jit_solution(9673585787139765644)
XLA Ops:
  0.6 0.0 copy-start.1
  0.6 0.6 copy-done.1
  1.3 0.7 copy.9.owners
  2.0 94.8 %kfac.1 = (f32[48,768]{1,0:T(8,128)}, f32[48,1536]{1,0:T(8,128)}) custom-call(bf16[48,256]{1,0:T(8,128)(2,1)} %bitcast.8, bf16[48,256]{1,0:T(8,128)(2,1)} %bitcast.9, bf16[48,6144]{1,0:T(8,128)(2,1)} %ainv.1, bf16[48,3072]{1,0:T(8,128)(2,1)} %oinv.1, s32[128,1]{1,0:T(8,128)} %copy.9.owners, f32[48,1536]{1,0:T(8,128)} %bitcast.7, f32[48,768]{1,0:T(8,128)} %mom.1), custom_call_target="tpu_custom_call" | custom-call | flops 460000000 | bytes 2000000 | tf_op jit(solution)/shard_map/kfac/pallas_call | solution.py:359
  96.8 0.0 copy-start
  96.8 1.6 %copy.12 = f32[48,768]{1,0:T(8,128)} copy(f32[48,768]{1,0:T(8,128)} %get-tuple-element.8) | data formatting | bytes 294912
  98.5 0.0 copy-done
  98.5 0.7 copy.13
Async XLA Ops:
  0.6 0.7 copy-start.1
  96.8 1.6 %copy-start = (f32[48,1536]{1,0:T(8,128)S(1)}, f32[48,1536]{1,0:T(8,128)}, u32[]{:S(2)}) copy-start(f32[48,1536]{1,0:T(8,128)} %get-tuple-element.5) | copy-start | bytes 884740

commit v4 on v2

--- a/solution.py
+++ b/solution.py
@@ -20,8 +20,8 @@
 
 def kernel(
     at, gt, ainv, oinv, owners, fac, mom, out_m, out_f,
-    av, ow, fv, mv, ra, rg, lhs, an, ap, ai, oi, cvf, cs, cr, yp, yc, yhs, yhr, yb,
-    pp, pys, pyr, pa, pls, plr, pb, pbs, plp, pq, pf, mf, ms, mr,
+    av, ow, pk, fv, mv, ra, rg, lhs, an, ap, ai, oi, cvf, cs, cr, yp, yc, yhs, yhr, yb,
+    pg, pp, pys, pyr, pa, pls, plr, pb, pbs, plp, pq, pf, mf, ms, mr,
     loc, t0s, t0r, fws, fwr, zs, ys, lr, ais, air, ois, oir, cvs, cvr, yss, ysr,
     pyss, pysr, plss, plsr, pfzs, pfys, pfr, mss, msr,
 ):
@@ -142,8 +142,9 @@
         send(oi.at[r], oi.at[r], ois.at[k - 1], oir.at[k - 1], dev(x_=xk[k]))
 
     own[0].wait()
-    natural = lax.broadcasted_iota(jnp.int32, (32, 128), 1)
-    pick = jnp.where(ow[pl.ds(pl.multiple_of(g * 32, 8), 32), :] == natural, 1.0, 0.0).astype(BF)
+    natural = lax.broadcasted_iota(jnp.int32, (128, 128), 0)
+    pk[...] = jnp.where(ow[...] == natural, 1.0, 0.0).T
+    pick = pk[pl.ds(pl.multiple_of(g * 32, 8), 32), :].astype(BF)
     for j in range(BR):
         col = an[pl.ds(j, 128, stride=BR), :].astype(BF)
         ap[pl.ds(j, 32, stride=BR), :] = jnp.dot(pick, col, preferred_element_type=F32)
@@ -168,11 +169,13 @@
     for k in range(1, NX):
         arrived(oi.at[rows(x_from(k), BR)], oir.at[k - 1])
     gm = rg[...].astype(F32).T.astype(BF)
-    part = jnp.dot(gm, oi[...], preferred_element_type=F32)
-    pp[...] = part
-    pys[...] = part.astype(BF)
+    pg[...] = gm
     for k in range(1, NY):
+        b = rows(yk[k], 64)
+        pys[b, :] = jnp.dot(pg[b, :], oi[...], preferred_element_type=F32).astype(BF)
         send(pys.at[rows(yk[k], 64)], pyr.at[k - 1], pyss.at[k - 1], pysr.at[k - 1], dev(y_=yk[k]))
+
+    pp[...] = jnp.dot(pg[rows(y, 64), :], oi[...], preferred_element_type=F32)
 
     def to_y(i, n):
         s = lhs.at[rows(i, BR)]
@@ -198,7 +201,7 @@
 
     for k in range(1, NY):
         arrived(pyr.at[k - 1], pysr.at[k - 1])
-    acc = pp[rows(y, 64), :]
+    acc = pp[...]
     for k in range(1, NY):
         acc = acc + pyr[k - 1].astype(F32)
     pa[...] = acc
@@ -360,7 +363,8 @@
         out_specs=(vm, vm),
         scratch_shapes=[
             pltpu.VMEM((BR, 128 * BR), BF),
-            pltpu.VMEM((128, 1), jnp.int32),
+            pltpu.VMEM((1, 128), jnp.int32),
+            pltpu.VMEM((128, 128), F32),
             pltpu.VMEM((BR, SLAB), F32),
             pltpu.VMEM((BR, CG), F32),
             pltpu.VMEM((192, TK), BF),
@@ -378,7 +382,8 @@
             pltpu.VMEM((96, TK), BF),
             pltpu.VMEM((96, TK), BF),
             pltpu.VMEM((192, TK), BF),
-            pltpu.VMEM((TK, CG), F32),
+            pltpu.VMEM((TK, 192), BF),
+            pltpu.VMEM((64, CG), F32),
             pltpu.VMEM((TK, CG), BF),
             pltpu.VMEM((3, 64, CG), BF),
             pltpu.VMEM((64, CG), F32),
@@ -407,7 +412,7 @@
         ),
         name="kfac",
     )(
-        activations.T, output_grads.T, input_inverse, output_inverse, owner_table[:, None], factor_slab.T, momentum
+        activations.T, output_grads.T, input_inverse, output_inverse, owner_table[None, :], factor_slab.T, momentum
     )
     return (new_momentum, factor_t.T)
 

time: 71.5 us -> 70 us (0.979)
  local copies, waits for them, and re-layouts: 3.73 us -> 2.34 us
    broadcast_in_dim x1 -> x0, local copies, waits for them, and re-layouts: 0.74 us -> none  [shards(): owner_table[:, None]]
    unnamed x6 -> x4, local copies, waits for them, and re-layouts: 2.99 us -> 2.34 us
where the time goes in v4:
time: 70 us; the launch traced here: 69.8 us
  Pallas kernels  66.9 us (96%)
  local copies, waits for them, and re-layouts  2.34 us (3%)
    pallas_call x1, Pallas kernels, shards(): pl.pallas_call(kernel, out_shape=(jax.ShapeDtypeStruct((BR, CG), F32), ja...  66.9 us
    unnamed x4, local copies, waits for them, and re-layouts  2.34 us

profile of v4, /device:TPU:1, one launch (start us, length us, event | category | flops | bytes accessed | tf_op | source)
XLA Modules:
  0.0 69.8 jit_solution(7816633570162478372)
XLA Ops:
  0.6 66.9 %kfac.1 = (f32[48,768]{1,0:T(8,128)}, f32[48,1536]{1,0:T(8,128)}) custom-call(bf16[48,256]{1,0:T(8,128)(2,1)} %bitcast.7, bf16[48,256]{1,0:T(8,128)(2,1)} %bitcast.8, bf16[48,6144]{1,0:T(8,128)(2,1)} %ainv.1, bf16[48,3072]{1,0:T(8,128)(2,1)} %oinv.1, s32[1,128]{1,0:T(1,128)} %bitcast.9, f32[48,1536]{1,0:T(8,128)} %bitcast.6, f32[48,768]{1,0:T(8,128)} %mom.1), custom_call_target="tpu_custom_call" | custom-call | flops 460000000 | bytes 2000000 | tf_op jit(solution)/shard_map/kfac/pallas_call | solution.py:356
  67.5 0.0 copy-start
  67.5 1.6 %copy.11 = f32[48,768]{1,0:T(8,128)} copy(f32[48,768]{1,0:T(8,128)} %get-tuple-element.8) | data formatting | bytes 294912
  69.1 0.0 copy-done
  69.1 0.7 %copy.12 = f32[1536,48]{0,1:T(8,128)} copy(f32[1536,48]{0,1:T(8,128)S(1)} %bitcast.5) | data formatting | bytes 589824
Async XLA Ops:
  67.5 1.6 %copy-start = (f32[48,1536]{1,0:T(8,128)S(1)}, f32[48,1536]{1,0:T(8,128)}, u32[]{:S(2)}) copy-start(f32[48,1536]{1,0:T(8,128)} %get-tuple-element.5) | copy-start | bytes 884740

commit v5 on v4

--- a/solution.py
+++ b/solution.py
@@ -253,47 +253,12 @@
     for k in range(1, NY):
         send(pq, pf.at[r, q], pfys.at[0, k - 1], pfr.at[y * NL + l], dev(y_=yk[k]))
 
-    for j in range(1, NY):
-        yy = y_from(j)
-        for b in range(NL):
-            arrived(lhs.at[rows(yy * NL + b, BR)], lr.at[yy * NL + b])
-        y_part(j)
-    send(yp.at[rows(1 - c, 96)], yc, yss.at[0], ysr.at[0], dev(c_=1 - c))
-
-    def pf_to_y(i, n):
-        r, q = place(y, i)
-        for m in range(1, NY):
-            send(pf.at[r, q], pf.at[r, q], pfys.at[n, m - 1], pfr.at[y * NL + i], dev(y_=yk[m]))
-
-    r, q = place(y, lp)
-    arrived(pf.at[r, q], pfr.at[y * NL + lp])
-    for k in range(1, 4):
-        send(pf.at[r, q], pf.at[r, q], pfzs.at[3 + k], pfr.at[y * NL + lp], dev(l_=lq[k]))
-    pf_to_y(lp, 1)
-
-    arrived(yc, ysr.at[0])
-    keep = rows(c, 96)
-    ysum = yp[keep, :] + yc[...]
-    yhs[...] = ysum.astype(BF)
-    send(yhs, yhr, yss.at[1], ysr.at[1], dev(h_=1 - h))
-
-    for k in (1, 3, 2):
-        i = lq_from(k)
-        r, q = place(y, i)
-        arrived(pf.at[r, q], pfr.at[y * NL + i])
-        pf_to_y(i, 1 + k)
-    for k in (1, 3, 2):
-        i = lax.rem(lq_from(k) + 4, NL)
-        r, q = place(y, i)
-        arrived(pf.at[r, q], pfr.at[y * NL + i])
-        pf_to_y(i, 4 + k)
-
     other = ra.at[rows(c + 2 * (1 - h), BR)]
     arrived(other, t0r.at[0, 1 - h])
     send(other, other, fws.at[0, 1], fwr.at[0, 1 - h], dev(c_=1 - c))
     for j in range(2):
         arrived(ra.at[rows(1 - c + 2 * j, BR)], fwr.at[0, j])
-    for j in range(NY):
+    def cov_part(j):
         s = lanes(y_from(j), CH)
         f = lhs[rows(y_from(j), CH), :]
         cov = lax.dot_general(ra[...], f, (((1,), (1,)), ((), ())), preferred_element_type=F32)
@@ -304,6 +269,46 @@
                 cs.at[rows(xk[k], BR), s], cr.at[k - 1, :, s],
                 cvs.at[k - 1, j], cvr.at[k - 1, j], dev(x_=xk[k]),
             )
+
+    cov_part(0)
+    for j in range(1, NY):
+        yy = y_from(j)
+        for b in range(NL):
+            arrived(lhs.at[rows(yy * NL + b, BR)], lr.at[yy * NL + b])
+        y_part(j)
+        if j < NY - 1:
+            cov_part(j)
+    send(yp.at[rows(1 - c, 96)], yc, yss.at[0], ysr.at[0], dev(c_=1 - c))
+
+    def pf_to_y(i, n):
+        r, q = place(y, i)
+        for m in range(1, NY):
+            send(pf.at[r, q], pf.at[r, q], pfys.at[n, m - 1], pfr.at[y * NL + i], dev(y_=yk[m]))
+
+    r, q = place(y, lp)
+    arrived(pf.at[r, q], pfr.at[y * NL + lp])
+    for k in range(1, 4):
+        send(pf.at[r, q], pf.at[r, q], pfzs.at[3 + k], pfr.at[y * NL + lp], dev(l_=lq[k]))
+    pf_to_y(lp, 1)
+
+    arrived(yc, ysr.at[0])
+    keep = rows(c, 96)
+    ysum = yp[keep, :] + yc[...]
+    yhs[...] = ysum.astype(BF)
+    send(yhs, yhr, yss.at[1], ysr.at[1], dev(h_=1 - h))
+
+    cov_part(NY - 1)
+
+    for k in (1, 3, 2):
+        i = lq_from(k)
+        r, q = place(y, i)
+        arrived(pf.at[r, q], pfr.at[y * NL + i])
+        pf_to_y(i, 1 + k)
+    for k in (1, 3, 2):
+        i = lax.rem(lq_from(k) + 4, NL)
+        r, q = place(y, i)
+        arrived(pf.at[r, q], pfr.at[y * NL + i])
+        pf_to_y(i, 4 + k)
 
     arrived(yhr, ysr.at[1])
     yb[keep, :] = (ysum + yhr[...].astype(F32)).astype(BF)

time: 70 us -> 69.8 us (level)
  no operation moved by 1% of the time
where the time goes in v5:
time: 69.8 us; the launch traced here: 69.5 us
  Pallas kernels  66.5 us (95%)
  local copies, waits for them, and re-layouts  2.34 us (3%)
    pallas_call x1, Pallas kernels, shards(): pl.pallas_call(kernel, out_shape=(jax.ShapeDtypeStruct((BR, CG), F32), ja...  66.5 us
    unnamed x4, local copies, waits for them, and re-layouts  2.34 us

profile of v5, /device:TPU:1, one launch (start us, length us, event | category | flops | bytes accessed | tf_op | source)
XLA Modules:
  0.0 69.5 jit_solution(5074548516325583806)
XLA Ops:
  0.6 66.5 %kfac.1 = (f32[48,768]{1,0:T(8,128)}, f32[48,1536]{1,0:T(8,128)}) custom-call(bf16[48,256]{1,0:T(8,128)(2,1)} %bitcast.7, bf16[48,256]{1,0:T(8,128)(2,1)} %bitcast.8, bf16[48,6144]{1,0:T(8,128)(2,1)} %ainv.1, bf16[48,3072]{1,0:T(8,128)(2,1)} %oinv.1, s32[1,128]{1,0:T(1,128)} %bitcast.9, f32[48,1536]{1,0:T(8,128)} %bitcast.6, f32[48,768]{1,0:T(8,128)} %mom.1), custom_call_target="tpu_custom_call" | custom-call | flops 460000000 | bytes 2000000 | tf_op jit(solution)/shard_map/kfac/pallas_call | solution.py:361
  67.1 0.0 copy-start
  67.1 1.6 %copy.11 = f32[48,768]{1,0:T(8,128)} copy(f32[48,768]{1,0:T(8,128)} %get-tuple-element.8) | data formatting | bytes 294912
  68.8 0.0 copy-done
  68.8 0.7 %copy.12 = f32[1536,48]{0,1:T(8,128)} copy(f32[1536,48]{0,1:T(8,128)S(1)} %bitcast.5) | data formatting | bytes 589824
Async XLA Ops:
  67.1 1.6 %copy-start = (f32[48,1536]{1,0:T(8,128)S(1)}, f32[48,1536]{1,0:T(8,128)}, u32[]{:S(2)}) copy-start(f32[48,1536]{1,0:T(8,128)} %get-tuple-element.5) | copy-start | bytes 884740
